TPU v7x, 256 devices: a whole 4x4x8 slice. The times are simulated.
256 devices in a mesh: rows: 8 (over z), hidden: 32 (over x, y, core).
Axes of the slice: x: 4, y: 4, z: 8, core: 2. Of those that a mesh axis runs over, the one named last changes fastest.
Arguments:
- tokens: bfloat16 [1024, 8192], P('hidden', 'rows'), may hold values from -6 to 6
- snapshot: int32 [1024, 1], replicated, may hold values from 0 to 63; in each aligned block of 1024 rows (0 to 1023, 1024 to 2047, ...) at most 32 rows name the same one
- gate_weight: bfloat16 [8192, 28672], P('rows', 'hidden'), may hold values from -0.0625 to 0.0625
- up_weight: bfloat16 [8192, 28672], P('rows', 'hidden'), may hold values from -0.0625 to 0.0625
- down_weight: bfloat16 [28672, 8192], P('hidden', 'rows'), may hold values from -0.03125 to 0.03125
- adapter_input_maps: bfloat16 [64, 8192, 128], P('hidden', 'rows')
- adapter_middle_maps: bfloat16 [64, 2, 64, 28672], P(None, None, 'rows', 'hidden'), may hold values from -0.375 to 0.375
- down_input_map: bfloat16 [64, 64, 28672], P(None, 'rows', 'hidden')
- down_output_map: bfloat16 [64, 64, 8192], P('hidden', None, 'rows'), may hold values from -0.75 to 0.75
Outputs:
- mixed: bfloat16 [1024, 8192], P('hidden', 'rows')
Inputs may be any that keep to these rules, and one draw needn't show every extreme that they name: Every snapshot is named by at least one row and by at most 32 rows; some snapshot is named by exactly 32 rows.
All inputs are finite; a program needn't handle non-finite values.
Results may differ from a plain program's by a relative error of at most 0.033.
Values may be sent and summed in bfloat16 or wider, within the bound.
No kernel may reach another device: no remote copies, remote signals or barrier semaphores. Data moves between devices by JAX's collectives and lax.ppermute only.
A program may use at most 128 MiB of HBM per device.

v0:
```python
import jax
import jax.numpy as jnp
from jax import lax
from jax.sharding import PartitionSpec as P


def slot_tables(snapshot, snapshot_total, capacity):
    row_total = snapshot.shape[0]
    snap_owner = snapshot[:, 0]
    onehot = (snap_owner[:, None] == jnp.arange(snapshot_total, dtype=jnp.int32)[None, :]).astype(
        jnp.int32
    )
    before = jnp.cumsum(onehot, axis=0) - onehot
    slot_index = jnp.sum(before * onehot, axis=1)
    token_of = jnp.full((snapshot_total, capacity), row_total, jnp.int32)
    token_of = token_of.at[snap_owner, slot_index].set(jnp.arange(row_total, dtype=jnp.int32))
    return (snap_owner, slot_index, token_of)


def swiglu(paired):
    return (jax.nn.silu(paired[:, 0]) * paired[:, 1]).astype(jnp.bfloat16)


def per_device(
    tokens,
    snapshot,
    gate_weight,
    up_weight,
    down_weight,
    adapter_input_maps,
    adapter_middle_maps,
    down_input_map,
    down_output_map,
):
    row_index = lax.axis_index("rows")
    hidden_index = lax.axis_index("hidden")
    all_count = snapshot.shape[0]
    snapshot_total = adapter_middle_maps.shape[0]
    capacity = 2 * all_count // snapshot_total
    snapshot_local = adapter_input_maps.shape[0]
    rank_block_values = adapter_middle_maps.shape[2]
    rank_full = down_output_map.shape[1]
    snap_owner, slot_index, token_of = slot_tables(snapshot, snapshot_total, capacity)
    filled_flag = token_of < all_count
    clamped_index = jnp.minimum(token_of, all_count - 1)
    own_first = hidden_index * snapshot_local
    own_clamped = lax.dynamic_slice_in_dim(clamped_index, own_first, snapshot_local, 0)
    own_filled = lax.dynamic_slice_in_dim(filled_flag, own_first, snapshot_local, 0)
    own_tokens = lax.dynamic_slice_in_dim(token_of, own_first, snapshot_local, 0)
    gathered = lax.all_gather(tokens, "hidden", axis=0, tiled=True)
    picked_snapshot = jnp.where(
        own_filled[:, :, None], gathered[own_clamped], jnp.zeros((), gathered.dtype)
    )
    rank_partial_values = jnp.einsum(
        "leh,lhr->ler", picked_snapshot, adapter_input_maps, preferred_element_type=jnp.float32
    )
    rank_partial_values = rank_partial_values.reshape(snapshot_local, capacity, 2, rank_full)
    placed = jnp.zeros((snapshot_total, capacity, 2, rank_full), jnp.float32)
    placed = lax.dynamic_update_slice_in_dim(placed, rank_partial_values, own_first, 0)
    rank_total = lax.psum(placed, ("rows", "hidden"))
    rank_activation_values = lax.dynamic_slice_in_dim(
        rank_total, row_index * rank_block_values, rank_block_values, 3
    ).astype(jnp.bfloat16)
    halves = []
    for half_position in range(2):
        grouped_rows = jnp.einsum(
            "sck,skf->scf",
            rank_activation_values[:, :, half_position],
            adapter_middle_maps[:, half_position],
            preferred_element_type=jnp.float32,
        )
        halves.append(grouped_rows[snap_owner, slot_index])
    adapter_gate_up = jnp.stack(halves, axis=1)
    gate_term = jnp.dot(gathered, gate_weight, preferred_element_type=jnp.float32)
    up_term = jnp.dot(gathered, up_weight, preferred_element_type=jnp.float32)
    adapter_rows = adapter_gate_up
    summed = lax.psum(
        (jnp.stack([gate_term, up_term], axis=1) + adapter_rows).astype(jnp.bfloat16), "rows"
    ).astype(jnp.float32)
    hidden_all = swiglu(summed)
    rows_grouped = jnp.where(
        filled_flag[:, :, None], hidden_all[clamped_index], jnp.zeros((), hidden_all.dtype)
    )
    down_part = jnp.einsum(
        "scf,skf->sck", rows_grouped, down_input_map, preferred_element_type=jnp.float32
    )
    placed_down = jnp.zeros((snapshot_total, capacity, rank_full), jnp.float32)
    placed_down = lax.dynamic_update_slice_in_dim(
        placed_down, down_part, row_index * rank_block_values, 2
    )
    down_total = lax.psum(placed_down, ("rows", "hidden"))
    down_rank = lax.dynamic_slice_in_dim(down_total, own_first, snapshot_local, 0).astype(
        jnp.bfloat16
    )
    lifted = jnp.einsum(
        "sck,skd->scd", down_rank, down_output_map, preferred_element_type=jnp.float32
    )
    feature_width = lifted.shape[2]
    adapter_down = jnp.zeros((all_count + 1, feature_width), jnp.float32)
    adapter_down = adapter_down.at[own_tokens.reshape(-1)].add(lifted.reshape(-1, feature_width))[
        :all_count
    ]
    adapter_rows = adapter_down
    return lax.psum_scatter(
        (
            jnp.dot(hidden_all, down_weight, preferred_element_type=jnp.float32) + adapter_rows
        ).astype(jnp.bfloat16),
        "hidden",
        scatter_dimension=0,
        tiled=True,
    )


def solution(mesh):
    return jax.shard_map(
        per_device,
        mesh=mesh,
        in_specs=(
            P("hidden", "rows"),
            P(),
            P("rows", "hidden"),
            P("rows", "hidden"),
            P("hidden", "rows"),
            P("hidden", "rows", None),
            P(None, None, "rows", "hidden"),
            P(None, "rows", "hidden"),
            P("hidden", None, "rows"),
        ),
        out_specs=P("hidden", "rows"),
        check_vma=False,
    )
```

profile of v0, /device:TPU:2, one launch (start us, length us, event | category | flops | bytes accessed | tf_op | source)
XLA Modules:
  0.0 571.1 jit_solution(12695949925899009694)
XLA Ops:
  6.5 0.7 all-gather.2.cloned.1.call-update
  7.3 0.7 fusion.19
  8.0 18.0 %reduce-window.6 = s32[64,8,128]{2,1,0:T(8,128)S(1)} reduce-window(s32[64,8,128]{2,1,0:T(8,128)S(1)} %fusion.19, s32[]{:T(128)} %constant.16.clone.1), window={size=1x1x128 pad=0_0x0_0x127_0}, to_apply=%region_0.0 | reduce-window | flops 8323072 | bytes 524292 | tf_op jit(solution)/shard_map/reduce-window
  26.6 0.8 fusion.18
  27.3 0.7 shift-left_or_fusion
  28.1 0.7 multiply_reduce_fusion
  28.8 0.8 and_reduce_fusion
  29.6 4.3 scatter_custom_fusion.1
  34.4 26.9 %all-gather.2.cloned.1.call-done = bf16[1024,1024]{1,0:T(8,128)(2,1)} async-done(((bf16[32,1024]{1,0:T(8,128)(2,1)}), bf16[1024,1024]{1,0:T(8,128)(2,1)}) %all-gather.2.cloned.1.call-update) | async-done | bytes 2097168 | tf_op jit(solution)/shard_map/all_gather | solution.py:50
  61.4 2.7 gather_fusion
  64.5 2.5 broadcast_in_dim.49
  67.6 130.6 %all-reduce.5 = bf16[64,32,2,64]{1,3,0,2:T(8,128)(2,1)} all-reduce(f32[64,32,2,64]{1,3,0,2:T(8,128)} %constant_dynamic-update-slice_fusion), channel_id=1, replica_groups=mesh['rows'=8,'hidden'=32] {'rows','hidden'}, use_global_device_ids=true, to_apply=%region_4.5 | all-reduce | flops 262144 | bytes 1572864 | tf_op jit(solution)/shard_map/psum | solution.py:60
  198.2 1.0 dynamic-slice_convert_fusion
  199.2 5.5 fusion.12
  204.7 4.1 fusion.10
  208.8 19.8 %gather_fusion.1 = f32[1024,896]{1,0:T(8,128)} fusion(f32[64,32,896]{2,1,0:T(8,128)} %fusion.12, s32[1024]{0:T(1024)S(1)} %bitcast.78), kind=kCustom, calls=%fused_computation.1 | custom fusion | bytes 7348224 | tf_op jit(solution)/shard_map/gather | solution.py:72
  228.7 19.9 %gather_fusion.2 = f32[1024,896]{1,0:T(8,128)} fusion(f32[64,32,896]{2,1,0:T(8,128)} %fusion.10, s32[1024]{0:T(1024)S(1)} %bitcast.79), kind=kCustom, calls=%fused_computation.2 | custom fusion | bytes 7348224 | tf_op jit(solution)/shard_map/gather | solution.py:72
  248.5 4.6 convolution_bitcast_fusion
  253.2 2.3 convolution_bitcast_fusion.1
  255.5 0.8 copy-done.2
  256.3 2.1 fusion
  259.3 96.2 %all-reduce.4.cloned.1.call-done = bf16[1024,2,896]{2,0,1:T(8,128)(2,1)} async-done(((bf16[1024,2,896]{2,0,1:T(8,128)(2,1)}), bf16[1024,2,896]{2,0,1:T(8,128)(2,1)}) %all-reduce.4.cloned.1.call-update) | async-done | bytes 3670032 | tf_op jit(solution)/shard_map/psum | solution.py:77
  355.5 2.5 convert_element_type.29
  358.0 2.3 fusion.3
  360.3 12.3 %gather_fusion.3 = bf16[2048,896]{1,0:T(8,128)(2,1)} fusion(bf16[1024,896]{1,0:T(8,128)(2,1)} %fusion.3, s32[2048]{0:T(1024)S(1)} %broadcast_clamp_fusion), kind=kCustom, calls=%fused_computation.3 | custom fusion | bytes 7348224 | tf_op jit(solution)/shard_map/gather | solution.py:82
  372.6 4.2 fusion.4
  376.9 5.2 dynamic_update_slice.7
  382.0 86.1 %all-reduce.6 = bf16[64,32,64]{2,1,0:T(8,128)(2,1)S(1)} all-reduce(f32[64,32,64]{2,1,0:T(8,128)S(1)} %dynamic_update_slice.7), channel_id=1, replica_groups=mesh['rows'=8,'hidden'=32] {'rows','hidden'}, use_global_device_ids=true, to_apply=%region_6.7 | all-reduce | flops 131072 | bytes 786432 | tf_op jit(solution)/shard_map/psum | solution.py:91
  468.1 1.1 fusion.24
  469.2 3.3 scatter_custom_fusion
  472.5 6.4 %fusion.1 = bf16[1024,1024]{1,0:T(8,128)(2,1)} fusion(f32[1025,1024]{1,0:T(8,128)} %scatter_custom_fusion, bf16[1024,896]{1,0:T(8,128)(2,1)} %fusion.3, bf16[896,1024]{1,0:T(8,128)(2,1)S(1)} %copy-done), kind=kOutput, calls=%fused_computation.9 | convolution fusion | flops 1881145344 | bytes 9961472 | tf_op jit(solution)/shard_map/dot_general | solution.py:106
  478.9 85.7 %reduce-scatter.2.cloned.1.call-done = bf16[32,1024]{1,0:T(8,128)(2,1)} async-done(((bf16[1024,1024]{1,0:T(8,128)(2,1)}), bf16[32,1024]{1,0:T(8,128)(2,1)}) %reduce-scatter.2.cloned.1.call-update) | async-done | bytes 65552 | tf_op jit(solution)/shard_map/reduce_scatter | solution.py:104
  (52 shorter events, 3.1 us)
Async XLA Ops:
  6.5 466.0 %copy-start = (bf16[896,1024]{1,0:T(8,128)(2,1)S(1)}, bf16[896,1024]{1,0:T(8,128)(2,1)}, u32[]{:S(2)}) copy-start(bf16[896,1024]{1,0:T(8,128)(2,1)} %param.13) | copy-start | bytes 5505028
  6.5 57.5 %copy-start.5 = (bf16[2,1024,128]{2,1,0:T(8,128)(2,1)S(1)}, bf16[2,1024,128]{2,1,0:T(8,128)(2,1)}, u32[]{:S(2)}) copy-start(bf16[2,1024,128]{2,1,0:T(8,128)(2,1)} %param.14) | copy-start | bytes 1572868
  6.5 54.8 %all-gather.2.cloned.1.call-start = ((), (), s32[]{:S(2)}) async-start(), calls=%async_computation.1 | async-start | bytes 2162688 | tf_op jit(solution)/shard_map/all_gather | solution.py:50
  7.3 348.2 %all-reduce.4.cloned.1.call-start = ((), (), s32[]{:S(2)}) async-start(), calls=%async_computation.2 | async-start | bytes 7340032 | tf_op jit(solution)/shard_map/psum | solution.py:77
  199.2 5.5 copy-start.3
  248.5 4.6 copy-start.4
  248.5 4.6 copy-start.6
  253.2 2.3 copy-start.1
  253.2 3.2 copy-start.2
  258.5 306.1 %reduce-scatter.2.cloned.1.call-start = ((), (), s32[]{:S(2)}) async-start(), calls=%async_computation.3 | async-start | bytes 2162688 | tf_op jit(solution)/shard_map/reduce_scatter | solution.py:104
  360.3 12.3 %copy-start.7 = (bf16[64,8,896]{2,1,0:T(8,128)(2,1)S(1)}, bf16[64,8,896]{2,1,0:T(8,128)(2,1)}, u32[]{:S(2)}) copy-start(bf16[64,8,896]{2,1,0:T(8,128)(2,1)} %param.16) | copy-start | bytes 2752516
Sparse Core Ops, SparseCore 0:
  9.9 51.3 all-gather.1
  258.6 96.7 all-reduce.3
  479.0 85.4 reduce-scatter.1
where the time goes:
time: 572 us; the launch traced here: 571 us
  blocking collectives  217 us (38%)
  waiting for transfers between devices  210 us (37%)
  local copies, waits for them, and re-layouts  70.6 us (12%)
  other arithmetic  32.2 us (6%)
  matrix products  28.5 us (5%)
  between operations  13.3 us (2%)
    psum x1, blocking collectives, per_device(): rank_total = lax.psum(placed, ('rows', 'hidden'))  131 us
    psum x1, waiting for transfers between devices, per_device(): lax.psum((jnp.stack([gate_term, up_term], axis=1) + adapter_rows).astype(...  96.2 us
    psum x1, blocking collectives, per_device(): down_total = lax.psum(placed_down, ('rows', 'hidden'))  86.1 us
    reduce_scatter x1, waiting for transfers between devices, per_device(): lax.psum_scatter((jnp.dot(hidden_all, down_weight, preferred_element_type...  85.7 us
    gather x2, local copies, waits for them, and re-layouts, per_device(): halves.append(grouped_rows[snap_owner, slot_index])  39.7 us
    all_gather x1, waiting for transfers between devices, per_device(): gathered = lax.all_gather(tokens, 'hidden', axis=0, tiled=True)  26.9 us
    another operation x3, other arithmetic  18.2 us
    gather x1, local copies, waits for them, and re-layouts, per_device(): hidden_all[clamped_index]  12.3 us
  transfers between devices with their start and end apart: 3, of which 3 were waited for; matrix products, arithmetic and copies ran while one was open for 5% of the time, Pallas kernels for 0%

commit v1 on v0

--- a/solution.py
+++ b/solution.py
@@ -57,7 +57,7 @@
     rank_partial_values = rank_partial_values.reshape(snapshot_local, capacity, 2, rank_full)
     placed = jnp.zeros((snapshot_total, capacity, 2, rank_full), jnp.float32)
     placed = lax.dynamic_update_slice_in_dim(placed, rank_partial_values, own_first, 0)
-    rank_total = lax.psum(placed, ("rows", "hidden"))
+    rank_total = lax.psum(lax.psum(placed, "hidden"), "rows")
     rank_activation_values = lax.dynamic_slice_in_dim(
         rank_total, row_index * rank_block_values, rank_block_values, 3
     ).astype(jnp.bfloat16)

time: 572 us -> 652 us (1.14)
  waiting for transfers between devices: 210 us -> 321 us
  blocking collectives: 217 us -> 176 us
    psum x0 -> x1, waiting for transfers between devices: none -> 110 us  [per_device(): rank_total = lax.psum(lax.psum(placed, 'hidden'), 'rows')]
    psum x1, blocking collectives: 131 us -> 90.4 us  [per_device(): rank_total = lax.psum(lax.psum(placed, 'hidden'), 'rows')]
  transfers between devices with their start and end apart: 3 -> 4, of which waited for: 3 -> 4; matrix products, arithmetic and copies ran while one was open for 5% -> 6% of each run, Pallas kernels for 0% -> 0%
where the time goes in v1:
time: 652 us; the launch traced here: 650 us
  waiting for transfers between devices  321 us (49%)
  blocking collectives  176 us (27%)
  local copies, waits for them, and re-layouts  69.9 us (11%)
  other arithmetic  37.5 us (6%)
  matrix products  32.1 us (5%)
  between operations  13.3 us (2%)
    psum x1, waiting for transfers between devices, per_device(): rank_total = lax.psum(lax.psum(placed, 'hidden'), 'rows')  110 us
    psum x1, waiting for transfers between devices, per_device(): lax.psum((jnp.stack([gate_term, up_term], axis=1) + adapter_rows).astype(...  97.2 us
    psum x1, blocking collectives, per_device(): rank_total = lax.psum(lax.psum(placed, 'hidden'), 'rows')  90.4 us
    psum x1, blocking collectives, per_device(): down_total = lax.psum(placed_down, ('rows', 'hidden'))  86.1 us
    reduce_scatter x1, waiting for transfers between devices, per_device(): lax.psum_scatter((jnp.dot(hidden_all, down_weight, preferred_element_type...  85.7 us
    gather x2, local copies, waits for them, and re-layouts, per_device(): halves.append(grouped_rows[snap_owner, slot_index])  39.7 us
    all_gather x1, waiting for transfers between devices, per_device(): gathered = lax.all_gather(tokens, 'hidden', axis=0, tiled=True)  26.9 us
    another operation x3, other arithmetic  18.2 us
  transfers between devices with their start and end apart: 4, of which 4 were waited for; matrix products, arithmetic and copies ran while one was open for 6% of the time, Pallas kernels for 0%

profile of v1, /device:TPU:2, one launch (start us, length us, event | category | flops | bytes accessed | tf_op | source)
XLA Modules:
  0.0 650.5 jit_solution(17582307295862246170)
XLA Ops:
  6.5 0.7 all-gather.2.cloned.1.call-update
  7.3 0.7 fusion.19
  8.0 18.0 %reduce-window.6 = s32[64,8,128]{2,1,0:T(8,128)S(1)} reduce-window(s32[64,8,128]{2,1,0:T(8,128)S(1)} %fusion.19, s32[]{:T(128)} %constant.16.clone.1), window={size=1x1x128 pad=0_0x0_0x127_0}, to_apply=%region_0.0 | reduce-window | flops 8323072 | bytes 524292 | tf_op jit(solution)/shard_map/reduce-window
  26.6 0.8 fusion.18
  27.3 0.7 shift-left_or_fusion
  28.1 0.7 multiply_reduce_fusion
  28.8 0.8 and_reduce_fusion
  29.6 4.3 scatter_custom_fusion.1
  34.4 26.9 %all-gather.2.cloned.1.call-done = bf16[1024,1024]{1,0:T(8,128)(2,1)} async-done(((bf16[32,1024]{1,0:T(8,128)(2,1)}), bf16[1024,1024]{1,0:T(8,128)(2,1)}) %all-gather.2.cloned.1.call-update) | async-done | bytes 2097168 | tf_op jit(solution)/shard_map/all_gather | solution.py:50
  61.4 2.7 gather_fusion
  64.5 2.5 broadcast_in_dim.49
  67.7 6.4 convolution_bitcast_fusion
  74.1 4.2 convolution_bitcast_fusion.1
  78.3 110.3 %all-reduce.5.cloned.1.call-done = f32[64,32,2,64]{1,3,0,2:T(8,128)} async-done(((f32[64,32,2,64]{1,3,0,2:T(8,128)}), f32[64,32,2,64]{1,3,0,2:T(8,128)}) %all-reduce.5.cloned.1.call-update) | async-done | bytes 1048592 | tf_op jit(solution)/shard_map/psum | solution.py:60
  188.7 90.4 %all-reduce.8 = bf16[64,32,2,64]{1,3,0,2:T(8,128)(2,1)} all-reduce(f32[64,32,2,64]{1,3,0,2:T(8,128)} %all-reduce.5.cloned.1.call-done), channel_id=1, replica_groups=mesh['rows'=8,'hidden'=32] {'rows'}, use_global_device_ids=true, to_apply=%region_5.6 | all-reduce | flops 262144 | bytes 1572864 | tf_op jit(solution)/shard_map/psum | solution.py:60
  279.0 1.0 dynamic-slice_convert_fusion
  280.0 5.5 fusion.12
  285.5 4.1 fusion.10
  289.6 19.9 %gather_fusion.1 = f32[1024,896]{1,0:T(8,128)} fusion(f32[64,32,896]{2,1,0:T(8,128)} %fusion.12, s32[1024]{0:T(1024)S(1)} %bitcast.78), kind=kCustom, calls=%fused_computation.1 | custom fusion | bytes 7348224 | tf_op jit(solution)/shard_map/gather | solution.py:72
  309.5 19.9 %gather_fusion.2 = f32[1024,896]{1,0:T(8,128)} fusion(f32[64,32,896]{2,1,0:T(8,128)} %fusion.10, s32[1024]{0:T(1024)S(1)} %bitcast.79), kind=kCustom, calls=%fused_computation.2 | custom fusion | bytes 7348224 | tf_op jit(solution)/shard_map/gather | solution.py:72
  329.4 7.5 %fusion = bf16[1024,2,896]{2,0,1:T(8,128)(2,1)} fusion(f32[1024,1,896]{2,0,1:T(8,128)} %convolution_bitcast_fusion, f32[1024,1,896]{2,0,1:T(8,128)} %convolution_bitcast_fusion.1, f32[1024,1,896]{2,0,1:T(8,128)} %bitcast.81, f32[1024,1,896]{2,0,1:T(8,128)} %bitcast.80), kind=kLoop, calls=%fused_computation.7 | loop fusion | flops 7340032 | bytes 18350080 | tf_op jit(solution)/shard_map/convert_element_type | solution.py:78
  337.6 97.2 %all-reduce.7.cloned.1.call-done = bf16[1024,2,896]{2,0,1:T(8,128)(2,1)} async-done(((bf16[1024,2,896]{2,0,1:T(8,128)(2,1)}), bf16[1024,2,896]{2,0,1:T(8,128)(2,1)}) %all-reduce.7.cloned.1.call-update) | async-done | bytes 3670032 | tf_op jit(solution)/shard_map/psum | solution.py:77
  434.8 2.5 convert_element_type.29
  437.3 2.3 fusion.3
  439.6 12.3 %gather_fusion.3 = bf16[2048,896]{1,0:T(8,128)(2,1)} fusion(bf16[1024,896]{1,0:T(8,128)(2,1)} %fusion.3, s32[2048]{0:T(1024)S(1)} %broadcast_clamp_fusion), kind=kCustom, calls=%fused_computation.3 | custom fusion | bytes 7348224 | tf_op jit(solution)/shard_map/gather | solution.py:82
  451.9 4.2 fusion.4
  456.2 5.2 dynamic_update_slice.7
  461.3 86.1 %all-reduce.9 = bf16[64,32,64]{2,1,0:T(8,128)(2,1)S(1)} all-reduce(f32[64,32,64]{2,1,0:T(8,128)S(1)} %dynamic_update_slice.7), channel_id=1, replica_groups=mesh['rows'=8,'hidden'=32] {'rows','hidden'}, use_global_device_ids=true, to_apply=%region_7.8 | all-reduce | flops 131072 | bytes 786432 | tf_op jit(solution)/shard_map/psum | solution.py:91
  547.5 1.1 fusion.24
  548.6 3.3 scatter_custom_fusion
  551.8 6.4 fusion.1
  558.3 85.7 %reduce-scatter.2.cloned.1.call-done = bf16[32,1024]{1,0:T(8,128)(2,1)} async-done(((bf16[1024,1024]{1,0:T(8,128)(2,1)}), bf16[32,1024]{1,0:T(8,128)(2,1)}) %reduce-scatter.2.cloned.1.call-update) | async-done | bytes 65552 | tf_op jit(solution)/shard_map/reduce_scatter | solution.py:104
  (51 shorter events, 3.2 us)
Async XLA Ops:
  6.5 545.3 %copy-start = (bf16[896,1024]{1,0:T(8,128)(2,1)S(1)}, bf16[896,1024]{1,0:T(8,128)(2,1)}, u32[]{:S(2)}) copy-start(bf16[896,1024]{1,0:T(8,128)(2,1)} %param.13) | copy-start | bytes 5505028
  6.5 57.5 %copy-start.3 = (bf16[2,1024,128]{2,1,0:T(8,128)(2,1)S(1)}, bf16[2,1024,128]{2,1,0:T(8,128)(2,1)}, u32[]{:S(2)}) copy-start(bf16[2,1024,128]{2,1,0:T(8,128)(2,1)} %param.14) | copy-start | bytes 1572868
  6.5 54.8 %all-gather.2.cloned.1.call-start = ((), (), s32[]{:S(2)}) async-start(), calls=%async_computation.1 | async-start | bytes 2162688 | tf_op jit(solution)/shard_map/all_gather | solution.py:50
  7.3 181.4 %all-reduce.5.cloned.1.call-start = ((), (), s32[]{:S(2)}) async-start(), calls=%async_computation.2 | async-start | bytes 8388608 | tf_op jit(solution)/shard_map/psum | solution.py:60
  67.7 367.1 %all-reduce.7.cloned.1.call-start = ((), (), s32[]{:S(2)}) async-start(), calls=%async_computation.3 | async-start | bytes 7340032 | tf_op jit(solution)/shard_map/psum | solution.py:77
  67.7 6.4 copy-start.2
  67.7 6.4 copy-start.4
  280.0 5.5 copy-start.1
  336.9 307.1 %reduce-scatter.2.cloned.1.call-start = ((), (), s32[]{:S(2)}) async-start(), calls=%async_computation.4 | async-start | bytes 2162688 | tf_op jit(solution)/shard_map/reduce_scatter | solution.py:104
  439.6 12.3 %copy-start.5 = (bf16[64,8,896]{2,1,0:T(8,128)(2,1)S(1)}, bf16[64,8,896]{2,1,0:T(8,128)(2,1)}, u32[]{:S(2)}) copy-start(bf16[64,8,896]{2,1,0:T(8,128)(2,1)} %param.16) | copy-start | bytes 2752516
Sparse Core Ops, SparseCore 0:
  9.9 51.3 all-gather.1
  67.8 120.8 all-reduce.4
  337.0 97.7 all-reduce.6
  558.4 85.4 reduce-scatter.1
